TPU v7x, 32 devices: a whole 2x2x4 slice. The times are simulated.
32 devices in a mesh: sub: 16 (over z, y, x), rhs: 2 (over core).
Axes of the slice: x: 2, y: 2, z: 4, core: 2. Of those that a mesh axis runs over, the one named last changes fastest.
Arguments:
- schur_block: bfloat16 [32, 1024, 1024], P('sub', 'rhs'), may hold values from -1 to 4, as said below
- scaling: float32 [32, 1024], P('sub'), may hold values from 0.25 to 1.75
- gravity_load: float32 [32, 1024, 256], P('sub', None, 'rhs'), may hold values from -100 to 100
- pressure: bfloat16 [1024, 4, 256], P('sub', None, 'rhs'), may hold values from -6 to 6
- block_target: int32 [1024, 1], P('sub'), may hold values from 0 to 31; in each aligned block of 64 rows (0 to 63, 64 to 127, ...) at most 4 rows name the same one
- aero_interp: float32 [4, 1024], replicated, may hold values from -0.5 to 0.5
- partner_slot: int32 [4, 32], P(None, 'sub'), may hold values from 0 to 1, as said below
- corner_row: int32 [32, 8], P('sub'), may hold values from 0 to 1023
- corner_coarse: int32 [32, 8], P('sub'), may hold values from 0 to 127
- coarse_inverse: float32 [128, 128], P('sub'), may hold values from -1 to 6, as said below
Outputs:
- solution: float32 [32, 1024, 256], P('sub', None, 'rhs')
Inputs may be any that keep to these rules, and one draw needn't show every extreme that they name: `block_target`: at most 4 of the blocks of one device name the same subdomain; in some device's blocks one subdomain is named exactly 4 times; every subdomain is named by some block. In round k, subdomain s on device d = s // 2 is paired with subdomain (d xor 2^k) * 2 + partner_slot[k, s]; the pairing is mutual. `schur_block`: each matrix is symmetric. `coarse_inverse`: symmetric.
All inputs are finite; a program needn't handle non-finite values.
Results may differ from a plain program's by a relative error of at most 0.0027.
Values may be sent and summed in bfloat16 or wider, within the bound.
A program may use at most 64 MiB of HBM per device.

v0:
```python
import jax
import jax.numpy as jnp
from jax import lax
from jax.sharding import PartitionSpec as P

SUB_DEV = 2
FACES = 4
MOST = 4
ITERS = 2
FW = 256
coupling = 2.0


def swapped(shard, axis, distance):
    return lax.ppermute(shard, axis, [(i, i ^ 1 << distance) for i in range(lax.axis_size(axis))])


def all_sum(value):
    distance = 0
    while 1 << distance < lax.axis_size("sub"):
        value = value + swapped(value, "sub", distance)
        distance += 1
    return value


def schur_apply(schur_block, rounded):
    half_rows = jnp.einsum(
        "snm,smc->snc",
        schur_block,
        lax.all_gather(rounded, "rhs", axis=2, tiled=True),
        preferred_element_type=jnp.float32,
    )
    return lax.all_to_all(half_rows, "rhs", split_axis=2, concat_axis=1, tiled=True)


def jump_terms(rounded, partner_slot):
    face_terms = []
    for face_index in range(FACES):
        own_face = rounded[:, face_index * FW : (face_index + 1) * FW, :]
        partner_face = swapped(own_face, "sub", face_index)
        select = (
            partner_slot[face_index][:, None] == jnp.arange(SUB_DEV, dtype=jnp.int32)[None, :]
        ).astype(jnp.bfloat16)
        picked = jnp.einsum("sj,jfc->sfc", select, partner_face, preferred_element_type=jnp.float32)
        face_terms.append(coupling * (own_face.astype(jnp.float32) - picked))
    return jnp.concatenate(face_terms, axis=1)


def operator(direction, schur_block, partner_slot):
    rounded = direction.astype(jnp.bfloat16)
    return schur_apply(schur_block, rounded) + jump_terms(rounded, partner_slot)


def coarse_solve(coarse, coarse_inverse):
    own_rows = jnp.dot(coarse_inverse, coarse, precision=lax.Precision.HIGHEST)
    start = lax.axis_index("sub") * own_rows.shape[0]
    whole = jnp.zeros_like(coarse)
    return all_sum(lax.dynamic_update_slice(whole, own_rows, (start, 0)))


def add_corners(solved, corner_row, corner_coarse, residual):
    sub_rows = jnp.arange(SUB_DEV, dtype=jnp.int32)[:, None]
    return jnp.zeros_like(residual).at[sub_rows, corner_row].add(solved[corner_coarse])


def precondition(residual, schur_block, scaling, corner_row, corner_coarse, coarse_inverse):
    columns = residual.shape[2]
    weight_col = scaling[:, :, None]
    dirichlet = weight_col * schur_apply(schur_block, (weight_col * residual).astype(jnp.bfloat16))
    sub_rows = jnp.arange(SUB_DEV, dtype=jnp.int32)[:, None]
    picked = residual[sub_rows, corner_row]
    partial_sum = (
        jnp.zeros((coarse_inverse.shape[1], columns), jnp.float32)
        .at[corner_coarse.reshape(-1)]
        .add(picked.reshape(-1, columns))
    )
    coarse = all_sum(partial_sum)
    solved = coarse_solve(coarse, coarse_inverse)
    precond = dirichlet + add_corners(solved, corner_row, corner_coarse, residual)
    product_value = all_sum(jnp.sum(residual * precond, axis=(0, 1)))
    return (precond, product_value)


def on_device(
    schur_block,
    scaling,
    gravity_load,
    pressure,
    block_target,
    aero_interp,
    partner_slot,
    corner_row,
    corner_coarse,
    coarse_inverse,
):
    sub_count = lax.axis_size("sub")
    all_subdomains = SUB_DEV * sub_count
    columns = gravity_load.shape[2]
    points = pressure.shape[1]
    target = block_target[:, 0]
    matches = target[:, None] == target[None, :]
    before = jnp.tril(matches, -1)
    rank_in = jnp.sum(before, axis=1, dtype=jnp.int32)
    slot_index = target * MOST + rank_in
    buffer = (
        jnp.zeros((all_subdomains * MOST, points, columns), jnp.bfloat16)
        .at[slot_index]
        .set(pressure)
    )
    arrived = lax.all_to_all(buffer, "sub", split_axis=0, concat_axis=0, tiled=True)
    load_sum = jnp.sum(
        arrived.reshape(sub_count, SUB_DEV, MOST, points, columns), axis=(0, 2), dtype=jnp.float32
    )
    force_total = gravity_load + jnp.einsum(
        "pm,spc->smc", aero_interp, load_sum, precision=lax.Precision.HIGHEST
    )
    solution = jnp.zeros_like(force_total)
    residual = force_total
    precond, precond_dot = precondition(
        residual, schur_block, scaling, corner_row, corner_coarse, coarse_inverse
    )
    direction = precond
    for step_index in range(ITERS):
        applied = operator(direction, schur_block, partner_slot)
        curvature = all_sum(jnp.sum(direction * applied, axis=(0, 1)))
        step_size = precond_dot / curvature
        solution = solution + step_size * direction
        residual = residual - step_size * applied
        if step_index + 1 < ITERS:
            precond, next_product = precondition(
                residual, schur_block, scaling, corner_row, corner_coarse, coarse_inverse
            )
            direction = precond + next_product / precond_dot * direction
            precond_dot = next_product
    return solution


def solution(mesh):
    return jax.shard_map(
        on_device,
        mesh=mesh,
        in_specs=(
            P("sub", "rhs", None),
            P("sub", None),
            P("sub", None, "rhs"),
            P("sub", None, "rhs"),
            P("sub", None),
            P(),
            P(None, "sub"),
            P("sub", None),
            P("sub", None),
            P("sub", None),
        ),
        out_specs=P("sub", None, "rhs"),
        check_vma=False,
    )
```

profile of v0, /device:TPU:0, one launch (start us, length us, event | category | flops | bytes accessed | tf_op | source)
XLA Modules:
  0.0 293.3 jit_solution(6070715701411228412)
XLA Ops:
  8.9 6.8 %scatter_fusion = bf16[128,4,128]{2,1,0:T(4,128)(2,1)} fusion(bf16[128,4,128]{2,1,0:T(4,128)(2,1)} %broadcast_in_dim.12, s32[64]{0:T(128)S(1)} %fusion.24, bf16[64,4,128]{2,1,0:T(4,128)(2,1)} %param.13), kind=kCustom, calls=%fused_computation.4 | custom fusion | bytes 196864 | tf_op jit(solution)/shard_map/scatter | solution.py:108
  15.7 8.4 %all-to-all-start = ((bf16[128,4,128]{2,1,0:T(4,128)(2,1)}), bf16[128,4,128]{2,1,0:T(4,128)(2,1)S(1)}, u32[]{:S(2)}, u32[]{:S(2)}) async-start(bf16[128,4,128]{2,1,0:T(4,128)(2,1)} %scatter_fusion), calls=%async_computation | async-start | bytes 262144 | tf_op jit(solution)/shard_map/all_to_all | solution.py:110
  24.8 2.5 copy.107
  27.5 4.4 %all-to-all-done = bf16[128,4,128]{2,1,0:T(4,128)(2,1)S(1)} async-done(((bf16[128,4,128]{2,1,0:T(4,128)(2,1)}), bf16[128,4,128]{2,1,0:T(4,128)(2,1)S(1)}, u32[]{:S(2)}, u32[]{:S(2)}) %all-to-all-start) | async-done | bytes 131104 | tf_op jit(solution)/shard_map/all_to_all | solution.py:110
  31.9 3.1 %multiply_convert_fusion.1 = (bf16[2,1024,128]{1,2,0:T(8,128)(2,1)}, f32[2,1024,128]{1,2,0:T(8,128)S(1)}) fusion(f32[2,1024]{1,0:T(2,128)S(1)} %copy-done.9, f32[2,1024,128]{1,2,0:T(8,128)} %copy.107, f32[2,4,128]{2,1,0:T(4,128)S(1)} %convert_reduce_fusion, f32[4,1024]{1,0:T(4,128)S(1)} %copy-done.12), kind=kOutput, calls=%fused_computation.32 | convolution fusion | flops 13369344 | bytes 2650112 | tf_op jit(solution)/shard_map/pm,spc->smc/dot_general | solution.py:114
  39.0 3.2 %collective-permute-done = f32[128,128]{1,0:T(8,128)S(1)} collective-permute-done((f32[128,128]{1,0:T(8,128)S(1)}, f32[128,128]{1,0:T(8,128)S(1)}, u32[]{:S(2)}, u32[]{:S(2)}) %collective-permute-start) | collective-permute-done | bytes 65568 | tf_op jit(solution)/shard_map/ppermute | solution.py:15
  43.0 3.5 %collective-permute-done.1 = f32[128,128]{1,0:T(8,128)S(1)} collective-permute-done((f32[128,128]{1,0:T(8,128)S(1)}, f32[128,128]{1,0:T(8,128)S(1)}, u32[]{:S(2)}, u32[]{:S(2)}) %collective-permute-start.1) | collective-permute-done | bytes 65568 | tf_op jit(solution)/shard_map/ppermute | solution.py:15
  47.4 3.8 %collective-permute-done.2 = f32[128,128]{1,0:T(8,128)S(1)} collective-permute-done((f32[128,128]{1,0:T(8,128)S(1)}, f32[128,128]{1,0:T(8,128)S(1)}, u32[]{:S(2)}, u32[]{:S(2)}) %collective-permute-start.2) | collective-permute-done | bytes 65568 | tf_op jit(solution)/shard_map/ppermute | solution.py:15
  52.0 5.0 %collective-permute-done.3 = f32[128,128]{1,0:T(8,128)S(1)} collective-permute-done((f32[128,128]{1,0:T(8,128)S(1)}, f32[128,128]{1,0:T(8,128)S(1)}, u32[]{:S(2)}, u32[]{:S(2)}) %collective-permute-start.3) | collective-permute-done | bytes 65568 | tf_op jit(solution)/shard_map/ppermute | solution.py:15
  58.0 3.4 %collective-permute-done.4 = f32[128,128]{1,0:T(8,128)S(1)} collective-permute-done((f32[128,128]{1,0:T(8,128)S(1)}, f32[128,128]{1,0:T(8,128)S(1)}, u32[]{:S(2)}, u32[]{:S(2)}) %collective-permute-start.4) | collective-permute-done | bytes 65568 | tf_op jit(solution)/shard_map/ppermute | solution.py:15
  62.2 3.5 %collective-permute-done.5 = f32[128,128]{1,0:T(8,128)S(1)} collective-permute-done((f32[128,128]{1,0:T(8,128)S(1)}, f32[128,128]{1,0:T(8,128)S(1)}, u32[]{:S(2)}, u32[]{:S(2)}) %collective-permute-start.5) | collective-permute-done | bytes 65568 | tf_op jit(solution)/shard_map/ppermute | solution.py:15
  66.0 4.1 %collective-permute-done.6 = f32[128,128]{1,0:T(8,128)S(1)} collective-permute-done((f32[128,128]{1,0:T(8,128)S(1)}, f32[128,128]{1,0:T(8,128)S(1)}, u32[]{:S(2)}, u32[]{:S(2)}) %collective-permute-start.6) | collective-permute-done | bytes 65568 | tf_op jit(solution)/shard_map/ppermute | solution.py:15
  70.4 5.1 %collective-permute-done.7 = f32[128,128]{1,0:T(8,128)S(1)} collective-permute-done((f32[128,128]{1,0:T(8,128)S(1)}, f32[128,128]{1,0:T(8,128)S(1)}, u32[]{:S(2)}, u32[]{:S(2)}) %collective-permute-start.7) | collective-permute-done | bytes 65568 | tf_op jit(solution)/shard_map/ppermute | solution.py:15
  78.9 4.6 %all_to_all.77 = f32[2,512,256]{1,0,2:T(2,128)S(1)} all-to-all(f32[2,512,256]{1,0,2:T(2,128)S(1)} %copy.108), channel_id=1, replica_groups=mesh['sub'=16,'rhs'=2] {'rhs'}, dimensions={2} | all-to-all | bytes 2097152 | tf_op jit(solution)/shard_map/all_to_all | solution.py:33
  119.4 4.6 %all_to_all.78 = f32[2,512,256]{1,0,2:T(2,128)S(1)} all-to-all(f32[2,512,256]{1,0,2:T(2,128)S(1)} %copy.114), channel_id=1, replica_groups=mesh['sub'=16,'rhs'=2] {'rhs'}, dimensions={2} | all-to-all | bytes 2097152 | tf_op jit(solution)/shard_map/all_to_all | solution.py:33
  125.8 3.1 %all_to_all.63 = f32[2,1024,128]{1,2,0:T(8,128)} reshape(f32[2,2,512,128]{2,1,3,0:T(2,128)} %bitcast.106) | data formatting | bytes 2097152 | tf_op jit(solution)/shard_map/all_to_all | solution.py:33
  149.2 2.5 copy.128
  154.6 3.1 %collective-permute-done.20 = f32[128,128]{1,0:T(8,128)S(1)} collective-permute-done((f32[128,128]{1,0:T(8,128)S(1)}, f32[128,128]{1,0:T(8,128)S(1)}, u32[]{:S(2)}, u32[]{:S(2)}) %collective-permute-start.20) | collective-permute-done | bytes 65568 | tf_op jit(solution)/shard_map/ppermute | solution.py:15
  158.9 3.1 %collective-permute-done.21 = f32[128,128]{1,0:T(8,128)S(1)} collective-permute-done((f32[128,128]{1,0:T(8,128)S(1)}, f32[128,128]{1,0:T(8,128)S(1)}, u32[]{:S(2)}, u32[]{:S(2)}) %collective-permute-start.21) | collective-permute-done | bytes 65568 | tf_op jit(solution)/shard_map/ppermute | solution.py:15
  163.5 2.8 collective-permute-done.22
  168.5 3.1 %collective-permute-done.23 = f32[128,128]{1,0:T(8,128)S(1)} collective-permute-done((f32[128,128]{1,0:T(8,128)S(1)}, f32[128,128]{1,0:T(8,128)S(1)}, u32[]{:S(2)}, u32[]{:S(2)}) %collective-permute-start.23) | collective-permute-done | bytes 65568 | tf_op jit(solution)/shard_map/ppermute | solution.py:15
  173.0 3.1 %collective-permute-done.24 = f32[128,128]{1,0:T(8,128)S(1)} collective-permute-done((f32[128,128]{1,0:T(8,128)S(1)}, f32[128,128]{1,0:T(8,128)S(1)}, u32[]{:S(2)}, u32[]{:S(2)}) %collective-permute-start.24) | collective-permute-done | bytes 65568 | tf_op jit(solution)/shard_map/ppermute | solution.py:15
  177.2 3.1 %collective-permute-done.25 = f32[128,128]{1,0:T(8,128)S(1)} collective-permute-done((f32[128,128]{1,0:T(8,128)S(1)}, f32[128,128]{1,0:T(8,128)S(1)}, u32[]{:S(2)}, u32[]{:S(2)}) %collective-permute-start.25) | collective-permute-done | bytes 65568 | tf_op jit(solution)/shard_map/ppermute | solution.py:15
  181.8 2.8 collective-permute-done.26
  186.8 3.1 %collective-permute-done.27 = f32[128,128]{1,0:T(8,128)S(1)} collective-permute-done((f32[128,128]{1,0:T(8,128)S(1)}, f32[128,128]{1,0:T(8,128)S(1)}, u32[]{:S(2)}, u32[]{:S(2)}) %collective-permute-start.27) | collective-permute-done | bytes 65568 | tf_op jit(solution)/shard_map/ppermute | solution.py:15
  193.4 4.6 %all_to_all.79 = f32[2,512,256]{1,0,2:T(2,128)S(1)} all-to-all(f32[2,512,256]{1,0,2:T(2,128)S(1)} %copy.126), channel_id=1, replica_groups=mesh['sub'=16,'rhs'=2] {'rhs'}, dimensions={2} | all-to-all | bytes 2097152 | tf_op jit(solution)/shard_map/all_to_all | solution.py:33
  199.8 3.1 %all_to_all.67 = f32[2,1024,128]{1,2,0:T(8,128)} reshape(f32[2,2,512,128]{2,1,3,0:T(2,128)} %bitcast.108) | data formatting | bytes 2097152 | tf_op jit(solution)/shard_map/all_to_all | solution.py:33
  205.3 2.5 copy.129
  210.0 2.6 copy.130
  256.2 4.6 %all_to_all.80 = f32[2,512,256]{1,0,2:T(2,128)S(1)} all-to-all(f32[2,512,256]{1,0,2:T(2,128)S(1)} %copy.133), channel_id=1, replica_groups=mesh['sub'=16,'rhs'=2] {'rhs'}, dimensions={2} | all-to-all | bytes 2097152 | tf_op jit(solution)/shard_map/all_to_all | solution.py:33
  262.5 3.1 %all_to_all.71 = f32[2,1024,128]{1,2,0:T(8,128)} reshape(f32[2,2,512,128]{2,1,3,0:T(2,128)} %bitcast.110) | data formatting | bytes 2097152 | tf_op jit(solution)/shard_map/all_to_all | solution.py:33
  280.2 2.7 collective-permute-done.39
  (226 shorter events, 161.1 us)
Async XLA Ops:
  15.7 16.2 %all-to-all-start = ((bf16[128,4,128]{2,1,0:T(4,128)(2,1)}), bf16[128,4,128]{2,1,0:T(4,128)(2,1)S(1)}, u32[]{:S(2)}, u32[]{:S(2)}) async-start(bf16[128,4,128]{2,1,0:T(4,128)(2,1)} %scatter_fusion), calls=%async_computation | async-start | bytes 262144 | tf_op jit(solution)/shard_map/all_to_all | solution.py:110
  24.0 52.0 %all-gather.5.cloned.1.call-start = ((), (), s32[]{:S(2)}) async-start(), calls=%async_computation.5 | async-start | bytes 1572864 | tf_op jit(solution)/shard_map/all_gather | solution.py:30
  37.8 4.3 %collective-permute-start = (f32[128,128]{1,0:T(8,128)S(1)}, f32[128,128]{1,0:T(8,128)S(1)}, u32[]{:S(2)}, u32[]{:S(2)}) collective-permute-start(f32[128,128]{1,0:T(8,128)S(1)} %scatter_custom_fusion.1), channel_id=1, source_target_pairs={{0,2},{2,0},{4,6},{6,4},{8,10},{10,8},{12,14},{14,12},{16,18},{18,... | collective-permute-start | bytes 196616 | tf_op jit(solution)/shard_map/ppermute | solution.py:15
  42.2 4.3 %collective-permute-start.1 = (f32[128,128]{1,0:T(8,128)S(1)}, f32[128,128]{1,0:T(8,128)S(1)}, u32[]{:S(2)}, u32[]{:S(2)}) collective-permute-start(f32[128,128]{1,0:T(8,128)S(1)} %add.182), channel_id=1, source_target_pairs={{0,4},{2,6},{4,0},{6,2},{8,12},{10,14},{12,8},{14,10},{16,20},{18,... | collective-permute-start | bytes 196616 | tf_op jit(solution)/shard_map/ppermute | solution.py:15
  46.5 4.7 %collective-permute-start.2 = (f32[128,128]{1,0:T(8,128)S(1)}, f32[128,128]{1,0:T(8,128)S(1)}, u32[]{:S(2)}, u32[]{:S(2)}) collective-permute-start(f32[128,128]{1,0:T(8,128)S(1)} %add.183), channel_id=1, source_target_pairs={{0,8},{2,10},{4,12},{6,14},{8,0},{10,2},{12,4},{14,6},{16,24},{18,... | collective-permute-start | bytes 196616 | tf_op jit(solution)/shard_map/ppermute | solution.py:15
  47.4 69.2 %all-gather.7.cloned.1.call-start = ((), (), s32[]{:S(2)}) async-start(), calls=%async_computation.6 | async-start | bytes 1572864 | tf_op jit(solution)/shard_map/all_gather | solution.py:30
  51.2 5.8 %collective-permute-start.3 = (f32[128,128]{1,0:T(8,128)S(1)}, f32[128,128]{1,0:T(8,128)S(1)}, u32[]{:S(2)}, u32[]{:S(2)}) collective-permute-start(f32[128,128]{1,0:T(8,128)S(1)} %add.184), channel_id=1, source_target_pairs={{0,16},{2,18},{4,20},{6,22},{8,24},{10,26},{12,28},{14,30},{16,0},... | collective-permute-start | bytes 196616 | tf_op jit(solution)/shard_map/ppermute | solution.py:15
  57.2 4.3 %collective-permute-start.4 = (f32[128,128]{1,0:T(8,128)S(1)}, f32[128,128]{1,0:T(8,128)S(1)}, u32[]{:S(2)}, u32[]{:S(2)}) collective-permute-start(f32[128,128]{1,0:T(8,128)S(1)} %get-tuple-element.37), channel_id=1, source_target_pairs={{0,2},{2,0},{4,6},{6,4},{8,10},{10,8},{12,14},{14,12},{16,18},{18,... | collective-permute-start | bytes 196616 | tf_op jit(solution)/shard_map/ppermute | solution.py:15
  61.4 4.3 %collective-permute-start.5 = (f32[128,128]{1,0:T(8,128)S(1)}, f32[128,128]{1,0:T(8,128)S(1)}, u32[]{:S(2)}, u32[]{:S(2)}) collective-permute-start(f32[128,128]{1,0:T(8,128)S(1)} %add_dynamic-update-slice_fusion.1), channel_id=1, source_target_pairs={{0,4},{2,6},{4,0},{6,2},{8,12},{10,14},{12,8},{14,10},{16,20},{18,... | collective-permute-start | bytes 196616 | tf_op jit(solution)/shard_map/ppermute | solution.py:15
  65.7 4.3 %collective-permute-start.6 = (f32[128,128]{1,0:T(8,128)S(1)}, f32[128,128]{1,0:T(8,128)S(1)}, u32[]{:S(2)}, u32[]{:S(2)}) collective-permute-start(f32[128,128]{1,0:T(8,128)S(1)} %add.188), channel_id=1, source_target_pairs={{0,8},{2,10},{4,12},{6,14},{8,0},{10,2},{12,4},{14,6},{16,24},{18,... | collective-permute-start | bytes 196616 | tf_op jit(solution)/shard_map/ppermute | solution.py:15
  70.1 5.4 %collective-permute-start.7 = (f32[128,128]{1,0:T(8,128)S(1)}, f32[128,128]{1,0:T(8,128)S(1)}, u32[]{:S(2)}, u32[]{:S(2)}) collective-permute-start(f32[128,128]{1,0:T(8,128)S(1)} %add.189), channel_id=1, source_target_pairs={{0,16},{2,18},{4,20},{6,22},{8,24},{10,26},{12,28},{14,30},{16,0},... | collective-permute-start | bytes 196616 | tf_op jit(solution)/shard_map/ppermute | solution.py:15
  95.4 5.5 %collective-permute-start.12 = (bf16[2,256,128]{1,2,0:T(8,128)(2,1)S(1)}, bf16[2,256,128]{1,2,0:T(8,128)(2,1)S(1)}, u32[]{:S(2)}, u32[]{:S(2)}) collective-permute-start(bf16[2,256,128]{1,2,0:T(8,128)(2,1)S(1)} %get-tuple-element.29), channel_id=1, source_target_pairs={{0,2},{2,0},{4,6},{6,4},{8,10},{10,8},{12,14},{14,12},{16,18},{18,... | collective-permute-start | bytes 393224 | tf_op jit(solution)/shard_map/ppermute | solution.py:15
  97.0 93.6 %all-gather.9.cloned.1.call-start = ((), (), s32[]{:S(2)}) async-start(), calls=%async_computation.7 | async-start | bytes 1572864 | tf_op jit(solution)/shard_map/all_gather | solution.py:30
  97.3 6.6 %collective-permute-start.13 = (bf16[2,256,128]{1,2,0:T(8,128)(2,1)}, bf16[2,256,128]{1,2,0:T(8,128)(2,1)}, u32[]{:S(2)}, u32[]{:S(2)}) collective-permute-start(bf16[2,256,128]{1,2,0:T(8,128)(2,1)} %get-tuple-element.32), channel_id=1, source_target_pairs={{0,4},{2,6},{4,0},{6,2},{8,12},{10,14},{12,8},{14,10},{16,20},{18,... | collective-permute-start | bytes 393224 | tf_op jit(solution)/shard_map/ppermute | solution.py:15
  97.8 9.8 %collective-permute-start.14 = (bf16[2,256,128]{1,2,0:T(8,128)(2,1)}, bf16[2,256,128]{1,2,0:T(8,128)(2,1)}, u32[]{:S(2)}, u32[]{:S(2)}) collective-permute-start(bf16[2,256,128]{1,2,0:T(8,128)(2,1)} %get-tuple-element.31), channel_id=1, source_target_pairs={{0,8},{2,10},{4,12},{6,14},{8,0},{10,2},{12,4},{14,6},{16,24},{18,... | collective-permute-start | bytes 393224 | tf_op jit(solution)/shard_map/ppermute | solution.py:15
  97.8 13.6 %collective-permute-start.15 = (bf16[2,256,128]{1,2,0:T(8,128)(2,1)}, bf16[2,256,128]{1,2,0:T(8,128)(2,1)S(1)}, u32[]{:S(2)}, u32[]{:S(2)}) collective-permute-start(bf16[2,256,128]{1,2,0:T(8,128)(2,1)} %get-tuple-element.30), channel_id=1, source_target_pairs={{0,16},{2,18},{4,20},{6,22},{8,24},{10,26},{12,28},{14,30},{16,0},... | collective-permute-start | bytes 393224 | tf_op jit(solution)/shard_map/ppermute | solution.py:15
  141.8 4.4 %collective-permute-start.19 = (f32[128]{0:T(128)S(1)}, f32[128]{0:T(128)S(1)}, u32[]{:S(2)}, u32[]{:S(2)}) collective-permute-start(f32[128]{0:T(128)S(1)} %add.199), channel_id=1, source_target_pairs={{0,16},{2,18},{4,20},{6,22},{8,24},{10,26},{12,28},{14,30},{16,0},... | collective-permute-start | bytes 1544 | tf_op jit(solution)/shard_map/ppermute | solution.py:15
  142.6 4.4 %collective-permute-start.11 = (f32[128]{0:T(128)S(1)}, f32[128]{0:T(128)S(1)}, u32[]{:S(2)}, u32[]{:S(2)}) collective-permute-start(f32[128]{0:T(128)S(1)} %add.194), channel_id=1, source_target_pairs={{0,16},{2,18},{4,20},{6,22},{8,24},{10,26},{12,28},{14,30},{16,0},... | collective-permute-start | bytes 1544 | tf_op jit(solution)/shard_map/ppermute | solution.py:15
  149.2 104.2 %all-gather.11.cloned.1.call-start = ((), (), s32[]{:S(2)}) async-start(), calls=%async_computation.8 | async-start | bytes 1572864 | tf_op jit(solution)/shard_map/all_gather | solution.py:30
  153.3 4.3 %collective-permute-start.20 = (f32[128,128]{1,0:T(8,128)S(1)}, f32[128,128]{1,0:T(8,128)S(1)}, u32[]{:S(2)}, u32[]{:S(2)}) collective-permute-start(f32[128,128]{1,0:T(8,128)S(1)} %scatter_custom_fusion.3), channel_id=1, source_target_pairs={{0,2},{2,0},{4,6},{6,4},{8,10},{10,8},{12,14},{14,12},{16,18},{18,... | collective-permute-start | bytes 196616 | tf_op jit(solution)/shard_map/ppermute | solution.py:15
  157.7 4.3 %collective-permute-start.21 = (f32[128,128]{1,0:T(8,128)S(1)}, f32[128,128]{1,0:T(8,128)S(1)}, u32[]{:S(2)}, u32[]{:S(2)}) collective-permute-start(f32[128,128]{1,0:T(8,128)S(1)} %add.201), channel_id=1, source_target_pairs={{0,4},{2,6},{4,0},{6,2},{8,12},{10,14},{12,8},{14,10},{16,20},{18,... | collective-permute-start | bytes 196616 | tf_op jit(solution)/shard_map/ppermute | solution.py:15
  162.0 4.3 %collective-permute-start.22 = (f32[128,128]{1,0:T(8,128)S(1)}, f32[128,128]{1,0:T(8,128)S(1)}, u32[]{:S(2)}, u32[]{:S(2)}) collective-permute-start(f32[128,128]{1,0:T(8,128)S(1)} %add.202), channel_id=1, source_target_pairs={{0,8},{2,10},{4,12},{6,14},{8,0},{10,2},{12,4},{14,6},{16,24},{18,... | collective-permute-start | bytes 196616 | tf_op jit(solution)/shard_map/ppermute | solution.py:15
  166.3 5.2 %collective-permute-start.23 = (f32[128,128]{1,0:T(8,128)S(1)}, f32[128,128]{1,0:T(8,128)S(1)}, u32[]{:S(2)}, u32[]{:S(2)}) collective-permute-start(f32[128,128]{1,0:T(8,128)S(1)} %add.203), channel_id=1, source_target_pairs={{0,16},{2,18},{4,20},{6,22},{8,24},{10,26},{12,28},{14,30},{16,0},... | collective-permute-start | bytes 196616 | tf_op jit(solution)/shard_map/ppermute | solution.py:15
  171.7 4.3 %collective-permute-start.24 = (f32[128,128]{1,0:T(8,128)S(1)}, f32[128,128]{1,0:T(8,128)S(1)}, u32[]{:S(2)}, u32[]{:S(2)}) collective-permute-start(f32[128,128]{1,0:T(8,128)S(1)} %get-tuple-element.39), channel_id=1, source_target_pairs={{0,2},{2,0},{4,6},{6,4},{8,10},{10,8},{12,14},{14,12},{16,18},{18,... | collective-permute-start | bytes 196616 | tf_op jit(solution)/shard_map/ppermute | solution.py:15
  180.3 4.3 %collective-permute-start.26 = (f32[128,128]{1,0:T(8,128)S(1)}, f32[128,128]{1,0:T(8,128)S(1)}, u32[]{:S(2)}, u32[]{:S(2)}) collective-permute-start(f32[128,128]{1,0:T(8,128)S(1)} %add.206), channel_id=1, source_target_pairs={{0,8},{2,10},{4,12},{6,14},{8,0},{10,2},{12,4},{14,6},{16,24},{18,... | collective-permute-start | bytes 196616 | tf_op jit(solution)/shard_map/ppermute | solution.py:15
  184.7 5.2 %collective-permute-start.27 = (f32[128,128]{1,0:T(8,128)S(1)}, f32[128,128]{1,0:T(8,128)S(1)}, u32[]{:S(2)}, u32[]{:S(2)}) collective-permute-start(f32[128,128]{1,0:T(8,128)S(1)} %add.207), channel_id=1, source_target_pairs={{0,16},{2,18},{4,20},{6,22},{8,24},{10,26},{12,28},{14,30},{16,0},... | collective-permute-start | bytes 196616 | tf_op jit(solution)/shard_map/ppermute | solution.py:15
  225.1 4.4 %collective-permute-start.31 = (f32[128]{0:T(128)S(1)}, f32[128]{0:T(128)S(1)}, u32[]{:S(2)}, u32[]{:S(2)}) collective-permute-start(f32[128]{0:T(128)S(1)} %add.211), channel_id=1, source_target_pairs={{0,16},{2,18},{4,20},{6,22},{8,24},{10,26},{12,28},{14,30},{16,0},... | collective-permute-start | bytes 1544 | tf_op jit(solution)/shard_map/ppermute | solution.py:15
  232.4 5.3 %collective-permute-start.32 = (bf16[2,256,128]{1,2,0:T(8,128)(2,1)S(1)}, bf16[2,256,128]{1,2,0:T(8,128)(2,1)S(1)}, u32[]{:S(2)}, u32[]{:S(2)}) collective-permute-start(bf16[2,256,128]{1,2,0:T(8,128)(2,1)S(1)} %get-tuple-element.21), channel_id=1, source_target_pairs={{0,2},{2,0},{4,6},{6,4},{8,10},{10,8},{12,14},{14,12},{16,18},{18,... | collective-permute-start | bytes 393224 | tf_op jit(solution)/shard_map/ppermute | solution.py:15
  233.6 7.0 %collective-permute-start.33 = (bf16[2,256,128]{1,2,0:T(8,128)(2,1)}, bf16[2,256,128]{1,2,0:T(8,128)(2,1)}, u32[]{:S(2)}, u32[]{:S(2)}) collective-permute-start(bf16[2,256,128]{1,2,0:T(8,128)(2,1)} %get-tuple-element.24), channel_id=1, source_target_pairs={{0,4},{2,6},{4,0},{6,2},{8,12},{10,14},{12,8},{14,10},{16,20},{18,... | collective-permute-start | bytes 393224 | tf_op jit(solution)/shard_map/ppermute | solution.py:15
  234.5 9.9 %collective-permute-start.34 = (bf16[2,256,128]{1,2,0:T(8,128)(2,1)}, bf16[2,256,128]{1,2,0:T(8,128)(2,1)}, u32[]{:S(2)}, u32[]{:S(2)}) collective-permute-start(bf16[2,256,128]{1,2,0:T(8,128)(2,1)} %get-tuple-element.23), channel_id=1, source_target_pairs={{0,8},{2,10},{4,12},{6,14},{8,0},{10,2},{12,4},{14,6},{16,24},{18,... | collective-permute-start | bytes 393224 | tf_op jit(solution)/shard_map/ppermute | solution.py:15
  236.3 11.9 %collective-permute-start.35 = (bf16[2,256,128]{1,2,0:T(8,128)(2,1)}, bf16[2,256,128]{1,2,0:T(8,128)(2,1)S(1)}, u32[]{:S(2)}, u32[]{:S(2)}) collective-permute-start(bf16[2,256,128]{1,2,0:T(8,128)(2,1)} %get-tuple-element.22), channel_id=1, source_target_pairs={{0,16},{2,18},{4,20},{6,22},{8,24},{10,26},{12,28},{14,30},{16,0},... | collective-permute-start | bytes 393224 | tf_op jit(solution)/shard_map/ppermute | solution.py:15
  278.5 4.4 %collective-permute-start.39 = (f32[128]{0:T(128)S(1)}, f32[128]{0:T(128)S(1)}, u32[]{:S(2)}, u32[]{:S(2)}) collective-permute-start(f32[128]{0:T(128)S(1)} %add.217), channel_id=1, source_target_pairs={{0,16},{2,18},{4,20},{6,22},{8,24},{10,26},{12,28},{14,30},{16,0},... | collective-permute-start | bytes 1544 | tf_op jit(solution)/shard_map/ppermute | solution.py:15
  (35 other events, 476.3 us)
Sparse Core Ops, SparseCore 0:
  47.5 6.6 all-gather.4
  97.2 7.4 all-gather.6
  149.3 7.6 all-gather.8
  233.7 9.0 all-gather.10
where the time goes:
time: 295 us; the launch traced here: 293 us
  waiting for transfers between devices  86.9 us (29%)
  local copies, waits for them, and re-layouts  67.7 us (23%)
  starting transfers between devices  55.6 us (19%)
  other arithmetic  29.9 us (10%)
  matrix products  21.3 us (7%)
  blocking collectives  18.3 us (6%)
  between operations  13.5 us (5%)
    ppermute x40, waiting for transfers between devices, swapped(): lax.ppermute(shard, axis, [(i, i ^ 1 << distance) for i in range(lax.axis...  82.5 us
    ppermute x40, starting transfers between devices, swapped(): lax.ppermute(shard, axis, [(i, i ^ 1 << distance) for i in range(lax.axis...  46.9 us
    all_to_all x4, blocking collectives, schur_apply(): lax.all_to_all(half_rows, 'rhs', split_axis=2, concat_axis=1, tiled=True)  18.3 us
    all_to_all x8, local copies, waits for them, and re-layouts, schur_apply(): lax.all_to_all(half_rows, 'rhs', split_axis=2, concat_axis=1, tiled=True)  17.4 us
    dot_general x8, matrix products, jump_terms(): jnp.einsum('sj,jfc->sfc', select, partner_face, preferred_element_type=jn...  10.1 us
    ppermute x8, local copies, waits for them, and re-layouts, swapped(): lax.ppermute(shard, axis, [(i, i ^ 1 << distance) for i in range(lax.axis...  9.77 us
    all_to_all x1, starting transfers between devices, on_device(): lax.all_to_all(buffer, 'sub', split_axis=0, concat_axis=0, tiled=True)  8.35 us
    dot_general x4, matrix products, schur_apply(): jnp.einsum('snm,smc->snc', schur_block, lax.all_gather(rounded, 'rhs', ax...  7.88 us
  transfers between devices with their start and end apart: 45, of which 34 were waited for; matrix products, arithmetic and copies ran while one was open for 14% of the time, Pallas kernels for 0%

commit v1 on v0

--- a/solution.py
+++ b/solution.py
@@ -9,6 +9,12 @@
 ITERS = 2
 FW = 256
 coupling = 2.0
+
+
+def stacked_exchange(value, axis, split, join):
+    cells = jnp.split(value, lax.axis_size(axis), axis=split)
+    received = lax.all_to_all(jnp.stack(cells), axis, 0, 0)
+    return jnp.concatenate(received, axis=join)
 
 
 def swapped(shard, axis, distance):
@@ -30,7 +36,7 @@
         lax.all_gather(rounded, "rhs", axis=2, tiled=True),
         preferred_element_type=jnp.float32,
     )
-    return lax.all_to_all(half_rows, "rhs", split_axis=2, concat_axis=1, tiled=True)
+    return stacked_exchange(half_rows, "rhs", 2, 1)
 
 
 def jump_terms(rounded, partner_slot):

time: 295 us -> 269 us (0.912)
  local copies, waits for them, and re-layouts: 67.7 us -> 47.7 us
  other arithmetic: 29.9 us -> 24.3 us
    all_to_all x8 -> x0, local copies, waits for them, and re-layouts: 17.4 us -> none  [schur_apply(): lax.all_to_all(half_rows, 'rhs', split_axis=2, concat_axis=1, tiled=True)]
    reduce_sum x2, other arithmetic: 4.38 us -> 0.78 us  [on_device(): curvature = all_sum(jnp.sum(direction * applied, axis=(0, 1)))]
    dot_general x4 -> x0, local copies, waits for them, and re-layouts: 3.24 us -> none  [schur_apply(): jnp.einsum('snm,smc->snc', schur_block, lax.all_gather(rounded, 'rhs', ax...]
  transfers between devices with their start and end apart: 45 -> 45, of which waited for: 34 -> 35; matrix products, arithmetic and copies ran while one was open for 14% -> 16% of each run, Pallas kernels for 0% -> 0%
where the time goes in v1:
time: 269 us; the launch traced here: 268 us
  waiting for transfers between devices  88.4 us (33%)
  starting transfers between devices  53.8 us (20%)
  local copies, waits for them, and re-layouts  47.7 us (18%)
  other arithmetic  24.3 us (9%)
  matrix products  21.3 us (8%)
  blocking collectives  18.6 us (7%)
  between operations  13.7 us (5%)
    ppermute x40, waiting for transfers between devices, swapped(): lax.ppermute(shard, axis, [(i, i ^ 1 << distance) for i in range(lax.axis...  83.9 us
    ppermute x40, starting transfers between devices, swapped(): lax.ppermute(shard, axis, [(i, i ^ 1 << distance) for i in range(lax.axis...  45.3 us
    all_to_all x4, blocking collectives, stacked_exchange(): received = lax.all_to_all(jnp.stack(cells), axis, 0, 0)  18.6 us
    dot_general x8, matrix products, jump_terms(): jnp.einsum('sj,jfc->sfc', select, partner_face, preferred_element_type=jn...  10.1 us
    ppermute x8, local copies, waits for them, and re-layouts, swapped(): lax.ppermute(shard, axis, [(i, i ^ 1 << distance) for i in range(lax.axis...  9.79 us
    all_to_all x1, starting transfers between devices, on_device(): lax.all_to_all(buffer, 'sub', split_axis=0, concat_axis=0, tiled=True)  8.38 us
    dot_general x4, matrix products, schur_apply(): jnp.einsum('snm,smc->snc', schur_block, lax.all_gather(rounded, 'rhs', ax...  7.88 us
    scatter x1, local copies, waits for them, and re-layouts, on_device(): buffer = jnp.zeros((all_subdomains * MOST, points, columns), jnp.bfloat16...  6.77 us
  transfers between devices with their start and end apart: 45, of which 35 were waited for; matrix products, arithmetic and copies ran while one was open for 16% of the time, Pallas kernels for 0%

profile of v1, /device:TPU:0, one launch (start us, length us, event | category | flops | bytes accessed | tf_op | source)
XLA Modules:
  0.0 267.8 jit_solution(15398155675783967642)
XLA Ops:
  8.9 6.8 %scatter_fusion = bf16[128,4,128]{2,1,0:T(4,128)(2,1)} fusion(bf16[128,4,128]{2,1,0:T(4,128)(2,1)} %broadcast_in_dim.12, s32[64]{0:T(128)S(1)} %fusion.24, bf16[64,4,128]{2,1,0:T(4,128)(2,1)} %param.13), kind=kCustom, calls=%fused_computation.4 | custom fusion | bytes 196864 | tf_op jit(solution)/shard_map/scatter | solution.py:114
  15.7 8.4 %all-to-all-start = ((bf16[128,4,128]{2,1,0:T(4,128)(2,1)}), bf16[128,4,128]{2,1,0:T(4,128)(2,1)S(1)}, u32[]{:S(2)}, u32[]{:S(2)}) async-start(bf16[128,4,128]{2,1,0:T(4,128)(2,1)} %scatter_fusion), calls=%async_computation | async-start | bytes 262144 | tf_op jit(solution)/shard_map/all_to_all | solution.py:116
  24.8 2.5 copy.70
  27.5 4.4 %all-to-all-done = bf16[128,4,128]{2,1,0:T(4,128)(2,1)S(1)} async-done(((bf16[128,4,128]{2,1,0:T(4,128)(2,1)}), bf16[128,4,128]{2,1,0:T(4,128)(2,1)S(1)}, u32[]{:S(2)}, u32[]{:S(2)}) %all-to-all-start) | async-done | bytes 131104 | tf_op jit(solution)/shard_map/all_to_all | solution.py:116
  32.0 3.1 %multiply_convert_fusion.1 = (bf16[2,1024,128]{1,2,0:T(8,128)(2,1)}, f32[2,1024,128]{1,2,0:T(8,128)S(1)}) fusion(f32[2,1024]{1,0:T(2,128)S(1)} %copy-done.11, f32[2,1024,128]{1,2,0:T(8,128)} %copy.70, f32[2,4,128]{2,1,0:T(4,128)S(1)} %convert_reduce_fusion, f32[4,1024]{1,0:T(4,128)S(1)} %copy-done.14), kind=kOutput, calls=%fused_computation.32 | convolution fusion | flops 13369344 | bytes 2650112 | tf_op jit(solution)/shard_map/pm,spc->smc/dot_general | solution.py:120
  39.0 3.2 %collective-permute-done = f32[128,128]{1,0:T(8,128)S(1)} collective-permute-done((f32[128,128]{1,0:T(8,128)S(1)}, f32[128,128]{1,0:T(8,128)S(1)}, u32[]{:S(2)}, u32[]{:S(2)}) %collective-permute-start) | collective-permute-done | bytes 65568 | tf_op jit(solution)/shard_map/ppermute | solution.py:21
  43.0 3.5 %collective-permute-done.1 = f32[128,128]{1,0:T(8,128)S(1)} collective-permute-done((f32[128,128]{1,0:T(8,128)S(1)}, f32[128,128]{1,0:T(8,128)S(1)}, u32[]{:S(2)}, u32[]{:S(2)}) %collective-permute-start.1) | collective-permute-done | bytes 65568 | tf_op jit(solution)/shard_map/ppermute | solution.py:21
  47.4 3.8 %collective-permute-done.2 = f32[128,128]{1,0:T(8,128)S(1)} collective-permute-done((f32[128,128]{1,0:T(8,128)S(1)}, f32[128,128]{1,0:T(8,128)S(1)}, u32[]{:S(2)}, u32[]{:S(2)}) %collective-permute-start.2) | collective-permute-done | bytes 65568 | tf_op jit(solution)/shard_map/ppermute | solution.py:21
  52.0 5.0 %collective-permute-done.3 = f32[128,128]{1,0:T(8,128)S(1)} collective-permute-done((f32[128,128]{1,0:T(8,128)S(1)}, f32[128,128]{1,0:T(8,128)S(1)}, u32[]{:S(2)}, u32[]{:S(2)}) %collective-permute-start.3) | collective-permute-done | bytes 65568 | tf_op jit(solution)/shard_map/ppermute | solution.py:21
  58.0 3.4 %collective-permute-done.4 = f32[128,128]{1,0:T(8,128)S(1)} collective-permute-done((f32[128,128]{1,0:T(8,128)S(1)}, f32[128,128]{1,0:T(8,128)S(1)}, u32[]{:S(2)}, u32[]{:S(2)}) %collective-permute-start.4) | collective-permute-done | bytes 65568 | tf_op jit(solution)/shard_map/ppermute | solution.py:21
  62.2 3.5 %collective-permute-done.5 = f32[128,128]{1,0:T(8,128)S(1)} collective-permute-done((f32[128,128]{1,0:T(8,128)S(1)}, f32[128,128]{1,0:T(8,128)S(1)}, u32[]{:S(2)}, u32[]{:S(2)}) %collective-permute-start.5) | collective-permute-done | bytes 65568 | tf_op jit(solution)/shard_map/ppermute | solution.py:21
  66.0 4.1 %collective-permute-done.6 = f32[128,128]{1,0:T(8,128)S(1)} collective-permute-done((f32[128,128]{1,0:T(8,128)S(1)}, f32[128,128]{1,0:T(8,128)S(1)}, u32[]{:S(2)}, u32[]{:S(2)}) %collective-permute-start.6) | collective-permute-done | bytes 65568 | tf_op jit(solution)/shard_map/ppermute | solution.py:21
  70.4 5.1 %collective-permute-done.7 = f32[128,128]{1,0:T(8,128)S(1)} collective-permute-done((f32[128,128]{1,0:T(8,128)S(1)}, f32[128,128]{1,0:T(8,128)S(1)}, u32[]{:S(2)}, u32[]{:S(2)}) %collective-permute-start.7) | collective-permute-done | bytes 65568 | tf_op jit(solution)/shard_map/ppermute | solution.py:21
  78.2 4.6 %all_to_all.25 = f32[2,2,512,128]{2,3,1,0:T(8,128)S(1)} all-to-all(f32[2,2,512,128]{2,3,1,0:T(8,128)S(1)} %pad_maximum_fusion), channel_id=1, replica_groups=mesh['sub'=16,'rhs'=2] {'rhs'}, dimensions={0} | all-to-all | bytes 2097152 | tf_op jit(solution)/shard_map/all_to_all | solution.py:16
  109.8 2.3 subtract_multiply_fusion.7
  114.4 4.7 %all_to_all.26 = f32[2,2,512,128]{2,3,1,0:T(8,128)S(1)} all-to-all(f32[2,2,512,128]{2,3,1,0:T(8,128)S(1)} %pad_maximum_fusion.1), channel_id=1, replica_groups=mesh['sub'=16,'rhs'=2] {'rhs'}, dimensions={0} | all-to-all | bytes 2097152 | tf_op jit(solution)/shard_map/all_to_all | solution.py:16
  137.6 2.6 copy.88
  143.1 3.1 %collective-permute-done.20 = f32[128,128]{1,0:T(8,128)S(1)} collective-permute-done((f32[128,128]{1,0:T(8,128)S(1)}, f32[128,128]{1,0:T(8,128)S(1)}, u32[]{:S(2)}, u32[]{:S(2)}) %collective-permute-start.20) | collective-permute-done | bytes 65568 | tf_op jit(solution)/shard_map/ppermute | solution.py:21
  147.5 3.1 %collective-permute-done.21 = f32[128,128]{1,0:T(8,128)S(1)} collective-permute-done((f32[128,128]{1,0:T(8,128)S(1)}, f32[128,128]{1,0:T(8,128)S(1)}, u32[]{:S(2)}, u32[]{:S(2)}) %collective-permute-start.21) | collective-permute-done | bytes 65568 | tf_op jit(solution)/shard_map/ppermute | solution.py:21
  152.1 2.8 %collective-permute-done.22 = f32[128,128]{1,0:T(8,128)S(1)} collective-permute-done((f32[128,128]{1,0:T(8,128)S(1)}, f32[128,128]{1,0:T(8,128)S(1)}, u32[]{:S(2)}, u32[]{:S(2)}) %collective-permute-start.22) | collective-permute-done | bytes 65568 | tf_op jit(solution)/shard_map/ppermute | solution.py:21
  157.1 3.1 %collective-permute-done.23 = f32[128,128]{1,0:T(8,128)S(1)} collective-permute-done((f32[128,128]{1,0:T(8,128)S(1)}, f32[128,128]{1,0:T(8,128)S(1)}, u32[]{:S(2)}, u32[]{:S(2)}) %collective-permute-start.23) | collective-permute-done | bytes 65568 | tf_op jit(solution)/shard_map/ppermute | solution.py:21
  161.5 3.1 %collective-permute-done.24 = f32[128,128]{1,0:T(8,128)S(1)} collective-permute-done((f32[128,128]{1,0:T(8,128)S(1)}, f32[128,128]{1,0:T(8,128)S(1)}, u32[]{:S(2)}, u32[]{:S(2)}) %collective-permute-start.24) | collective-permute-done | bytes 65568 | tf_op jit(solution)/shard_map/ppermute | solution.py:21
  165.8 3.1 %collective-permute-done.25 = f32[128,128]{1,0:T(8,128)S(1)} collective-permute-done((f32[128,128]{1,0:T(8,128)S(1)}, f32[128,128]{1,0:T(8,128)S(1)}, u32[]{:S(2)}, u32[]{:S(2)}) %collective-permute-start.25) | collective-permute-done | bytes 65568 | tf_op jit(solution)/shard_map/ppermute | solution.py:21
  170.4 2.8 %collective-permute-done.26 = f32[128,128]{1,0:T(8,128)S(1)} collective-permute-done((f32[128,128]{1,0:T(8,128)S(1)}, f32[128,128]{1,0:T(8,128)S(1)}, u32[]{:S(2)}, u32[]{:S(2)}) %collective-permute-start.26) | collective-permute-done | bytes 65568 | tf_op jit(solution)/shard_map/ppermute | solution.py:21
  175.4 3.1 %collective-permute-done.27 = f32[128,128]{1,0:T(8,128)S(1)} collective-permute-done((f32[128,128]{1,0:T(8,128)S(1)}, f32[128,128]{1,0:T(8,128)S(1)}, u32[]{:S(2)}, u32[]{:S(2)}) %collective-permute-start.27) | collective-permute-done | bytes 65568 | tf_op jit(solution)/shard_map/ppermute | solution.py:21
  181.3 4.6 %all_to_all.27 = f32[2,2,512,128]{2,3,1,0:T(8,128)S(1)} all-to-all(f32[2,2,512,128]{2,3,1,0:T(8,128)S(1)} %pad_maximum_fusion.2), channel_id=1, replica_groups=mesh['sub'=16,'rhs'=2] {'rhs'}, dimensions={0} | all-to-all | bytes 2097152 | tf_op jit(solution)/shard_map/all_to_all | solution.py:16
  187.1 2.5 copy.89
  191.9 2.5 copy.90
  201.0 2.4 collective-permute-done.29
  209.0 2.4 collective-permute-done.31
  237.1 4.7 %all_to_all.28 = f32[2,2,512,128]{2,3,1,0:T(8,128)S(1)} all-to-all(f32[2,2,512,128]{2,3,1,0:T(8,128)S(1)} %pad_maximum_fusion.3), channel_id=1, replica_groups=mesh['sub'=16,'rhs'=2] {'rhs'}, dimensions={0} | all-to-all | bytes 2097152 | tf_op jit(solution)/shard_map/all_to_all | solution.py:16
  258.8 2.5 copy.102
  (230 shorter events, 137.5 us)
Async XLA Ops:
  15.7 16.2 %all-to-all-start = ((bf16[128,4,128]{2,1,0:T(4,128)(2,1)}), bf16[128,4,128]{2,1,0:T(4,128)(2,1)S(1)}, u32[]{:S(2)}, u32[]{:S(2)}) async-start(bf16[128,4,128]{2,1,0:T(4,128)(2,1)} %scatter_fusion), calls=%async_computation | async-start | bytes 262144 | tf_op jit(solution)/shard_map/all_to_all | solution.py:116
  24.1 52.0 %all-gather.5.cloned.1.call-start = ((), (), s32[]{:S(2)}) async-start(), calls=%async_computation.5 | async-start | bytes 1572864 | tf_op jit(solution)/shard_map/all_gather | solution.py:36
  37.9 4.3 %collective-permute-start = (f32[128,128]{1,0:T(8,128)S(1)}, f32[128,128]{1,0:T(8,128)S(1)}, u32[]{:S(2)}, u32[]{:S(2)}) collective-permute-start(f32[128,128]{1,0:T(8,128)S(1)} %scatter_custom_fusion.1), channel_id=1, source_target_pairs={{0,2},{2,0},{4,6},{6,4},{8,10},{10,8},{12,14},{14,12},{16,18},{18,... | collective-permute-start | bytes 196616 | tf_op jit(solution)/shard_map/ppermute | solution.py:21
  42.2 4.3 %collective-permute-start.1 = (f32[128,128]{1,0:T(8,128)S(1)}, f32[128,128]{1,0:T(8,128)S(1)}, u32[]{:S(2)}, u32[]{:S(2)}) collective-permute-start(f32[128,128]{1,0:T(8,128)S(1)} %add.182), channel_id=1, source_target_pairs={{0,4},{2,6},{4,0},{6,2},{8,12},{10,14},{12,8},{14,10},{16,20},{18,... | collective-permute-start | bytes 196616 | tf_op jit(solution)/shard_map/ppermute | solution.py:21
  46.6 4.7 %collective-permute-start.2 = (f32[128,128]{1,0:T(8,128)S(1)}, f32[128,128]{1,0:T(8,128)S(1)}, u32[]{:S(2)}, u32[]{:S(2)}) collective-permute-start(f32[128,128]{1,0:T(8,128)S(1)} %add.183), channel_id=1, source_target_pairs={{0,8},{2,10},{4,12},{6,14},{8,0},{10,2},{12,4},{14,6},{16,24},{18,... | collective-permute-start | bytes 196616 | tf_op jit(solution)/shard_map/ppermute | solution.py:21
  47.4 64.8 %all-gather.7.cloned.1.call-start = ((), (), s32[]{:S(2)}) async-start(), calls=%async_computation.6 | async-start | bytes 1572864 | tf_op jit(solution)/shard_map/all_gather | solution.py:36
  51.2 5.8 %collective-permute-start.3 = (f32[128,128]{1,0:T(8,128)S(1)}, f32[128,128]{1,0:T(8,128)S(1)}, u32[]{:S(2)}, u32[]{:S(2)}) collective-permute-start(f32[128,128]{1,0:T(8,128)S(1)} %add.184), channel_id=1, source_target_pairs={{0,16},{2,18},{4,20},{6,22},{8,24},{10,26},{12,28},{14,30},{16,0},... | collective-permute-start | bytes 196616 | tf_op jit(solution)/shard_map/ppermute | solution.py:21
  57.2 4.3 %collective-permute-start.4 = (f32[128,128]{1,0:T(8,128)S(1)}, f32[128,128]{1,0:T(8,128)S(1)}, u32[]{:S(2)}, u32[]{:S(2)}) collective-permute-start(f32[128,128]{1,0:T(8,128)S(1)} %get-tuple-element.45), channel_id=1, source_target_pairs={{0,2},{2,0},{4,6},{6,4},{8,10},{10,8},{12,14},{14,12},{16,18},{18,... | collective-permute-start | bytes 196616 | tf_op jit(solution)/shard_map/ppermute | solution.py:21
  61.5 4.3 %collective-permute-start.5 = (f32[128,128]{1,0:T(8,128)S(1)}, f32[128,128]{1,0:T(8,128)S(1)}, u32[]{:S(2)}, u32[]{:S(2)}) collective-permute-start(f32[128,128]{1,0:T(8,128)S(1)} %add_dynamic-update-slice_fusion.1), channel_id=1, source_target_pairs={{0,4},{2,6},{4,0},{6,2},{8,12},{10,14},{12,8},{14,10},{16,20},{18,... | collective-permute-start | bytes 196616 | tf_op jit(solution)/shard_map/ppermute | solution.py:21
  65.8 4.3 %collective-permute-start.6 = (f32[128,128]{1,0:T(8,128)S(1)}, f32[128,128]{1,0:T(8,128)S(1)}, u32[]{:S(2)}, u32[]{:S(2)}) collective-permute-start(f32[128,128]{1,0:T(8,128)S(1)} %add.188), channel_id=1, source_target_pairs={{0,8},{2,10},{4,12},{6,14},{8,0},{10,2},{12,4},{14,6},{16,24},{18,... | collective-permute-start | bytes 196616 | tf_op jit(solution)/shard_map/ppermute | solution.py:21
  70.1 5.4 %collective-permute-start.7 = (f32[128,128]{1,0:T(8,128)S(1)}, f32[128,128]{1,0:T(8,128)S(1)}, u32[]{:S(2)}, u32[]{:S(2)}) collective-permute-start(f32[128,128]{1,0:T(8,128)S(1)} %add.189), channel_id=1, source_target_pairs={{0,16},{2,18},{4,20},{6,22},{8,24},{10,26},{12,28},{14,30},{16,0},... | collective-permute-start | bytes 196616 | tf_op jit(solution)/shard_map/ppermute | solution.py:21
  91.0 5.5 %collective-permute-start.12 = (bf16[2,256,128]{1,2,0:T(8,128)(2,1)S(1)}, bf16[2,256,128]{1,2,0:T(8,128)(2,1)S(1)}, u32[]{:S(2)}, u32[]{:S(2)}) collective-permute-start(bf16[2,256,128]{1,2,0:T(8,128)(2,1)S(1)} %get-tuple-element.37), channel_id=1, source_target_pairs={{0,2},{2,0},{4,6},{6,4},{8,10},{10,8},{12,14},{14,12},{16,18},{18,... | collective-permute-start | bytes 393224 | tf_op jit(solution)/shard_map/ppermute | solution.py:21
  92.6 86.6 %all-gather.9.cloned.1.call-start = ((), (), s32[]{:S(2)}) async-start(), calls=%async_computation.7 | async-start | bytes 1572864 | tf_op jit(solution)/shard_map/all_gather | solution.py:36
  92.7 6.7 %collective-permute-start.13 = (bf16[2,256,128]{1,2,0:T(8,128)(2,1)}, bf16[2,256,128]{1,2,0:T(8,128)(2,1)}, u32[]{:S(2)}, u32[]{:S(2)}) collective-permute-start(bf16[2,256,128]{1,2,0:T(8,128)(2,1)} %get-tuple-element.40), channel_id=1, source_target_pairs={{0,4},{2,6},{4,0},{6,2},{8,12},{10,14},{12,8},{14,10},{16,20},{18,... | collective-permute-start | bytes 393224 | tf_op jit(solution)/shard_map/ppermute | solution.py:21
  93.2 10.0 %collective-permute-start.14 = (bf16[2,256,128]{1,2,0:T(8,128)(2,1)}, bf16[2,256,128]{1,2,0:T(8,128)(2,1)}, u32[]{:S(2)}, u32[]{:S(2)}) collective-permute-start(bf16[2,256,128]{1,2,0:T(8,128)(2,1)} %get-tuple-element.39), channel_id=1, source_target_pairs={{0,8},{2,10},{4,12},{6,14},{8,0},{10,2},{12,4},{14,6},{16,24},{18,... | collective-permute-start | bytes 393224 | tf_op jit(solution)/shard_map/ppermute | solution.py:21
  93.2 13.8 %collective-permute-start.15 = (bf16[2,256,128]{1,2,0:T(8,128)(2,1)}, bf16[2,256,128]{1,2,0:T(8,128)(2,1)S(1)}, u32[]{:S(2)}, u32[]{:S(2)}) collective-permute-start(bf16[2,256,128]{1,2,0:T(8,128)(2,1)} %get-tuple-element.38), channel_id=1, source_target_pairs={{0,16},{2,18},{4,20},{6,22},{8,24},{10,26},{12,28},{14,30},{16,0},... | collective-permute-start | bytes 393224 | tf_op jit(solution)/shard_map/ppermute | solution.py:21
  130.3 4.4 %collective-permute-start.19 = (f32[128]{0:T(128)S(1)}, f32[128]{0:T(128)S(1)}, u32[]{:S(2)}, u32[]{:S(2)}) collective-permute-start(f32[128]{0:T(128)S(1)} %add.199), channel_id=1, source_target_pairs={{0,16},{2,18},{4,20},{6,22},{8,24},{10,26},{12,28},{14,30},{16,0},... | collective-permute-start | bytes 1544 | tf_op jit(solution)/shard_map/ppermute | solution.py:21
  131.1 4.4 %collective-permute-start.11 = (f32[128]{0:T(128)S(1)}, f32[128]{0:T(128)S(1)}, u32[]{:S(2)}, u32[]{:S(2)}) collective-permute-start(f32[128]{0:T(128)S(1)} %add.194), channel_id=1, source_target_pairs={{0,16},{2,18},{4,20},{6,22},{8,24},{10,26},{12,28},{14,30},{16,0},... | collective-permute-start | bytes 1544 | tf_op jit(solution)/shard_map/ppermute | solution.py:21
  137.5 97.3 %all-gather.11.cloned.1.call-start = ((), (), s32[]{:S(2)}) async-start(), calls=%async_computation.8 | async-start | bytes 1572864 | tf_op jit(solution)/shard_map/all_gather | solution.py:36
  141.9 4.3 %collective-permute-start.20 = (f32[128,128]{1,0:T(8,128)S(1)}, f32[128,128]{1,0:T(8,128)S(1)}, u32[]{:S(2)}, u32[]{:S(2)}) collective-permute-start(f32[128,128]{1,0:T(8,128)S(1)} %scatter_custom_fusion.3), channel_id=1, source_target_pairs={{0,2},{2,0},{4,6},{6,4},{8,10},{10,8},{12,14},{14,12},{16,18},{18,... | collective-permute-start | bytes 196616 | tf_op jit(solution)/shard_map/ppermute | solution.py:21
  146.2 4.3 %collective-permute-start.21 = (f32[128,128]{1,0:T(8,128)S(1)}, f32[128,128]{1,0:T(8,128)S(1)}, u32[]{:S(2)}, u32[]{:S(2)}) collective-permute-start(f32[128,128]{1,0:T(8,128)S(1)} %add.201), channel_id=1, source_target_pairs={{0,4},{2,6},{4,0},{6,2},{8,12},{10,14},{12,8},{14,10},{16,20},{18,... | collective-permute-start | bytes 196616 | tf_op jit(solution)/shard_map/ppermute | solution.py:21
  150.6 4.3 %collective-permute-start.22 = (f32[128,128]{1,0:T(8,128)S(1)}, f32[128,128]{1,0:T(8,128)S(1)}, u32[]{:S(2)}, u32[]{:S(2)}) collective-permute-start(f32[128,128]{1,0:T(8,128)S(1)} %add.202), channel_id=1, source_target_pairs={{0,8},{2,10},{4,12},{6,14},{8,0},{10,2},{12,4},{14,6},{16,24},{18,... | collective-permute-start | bytes 196616 | tf_op jit(solution)/shard_map/ppermute | solution.py:21
  154.9 5.2 %collective-permute-start.23 = (f32[128,128]{1,0:T(8,128)S(1)}, f32[128,128]{1,0:T(8,128)S(1)}, u32[]{:S(2)}, u32[]{:S(2)}) collective-permute-start(f32[128,128]{1,0:T(8,128)S(1)} %add.203), channel_id=1, source_target_pairs={{0,16},{2,18},{4,20},{6,22},{8,24},{10,26},{12,28},{14,30},{16,0},... | collective-permute-start | bytes 196616 | tf_op jit(solution)/shard_map/ppermute | solution.py:21
  160.3 4.3 %collective-permute-start.24 = (f32[128,128]{1,0:T(8,128)S(1)}, f32[128,128]{1,0:T(8,128)S(1)}, u32[]{:S(2)}, u32[]{:S(2)}) collective-permute-start(f32[128,128]{1,0:T(8,128)S(1)} %get-tuple-element.47), channel_id=1, source_target_pairs={{0,2},{2,0},{4,6},{6,4},{8,10},{10,8},{12,14},{14,12},{16,18},{18,... | collective-permute-start | bytes 196616 | tf_op jit(solution)/shard_map/ppermute | solution.py:21
  168.9 4.3 %collective-permute-start.26 = (f32[128,128]{1,0:T(8,128)S(1)}, f32[128,128]{1,0:T(8,128)S(1)}, u32[]{:S(2)}, u32[]{:S(2)}) collective-permute-start(f32[128,128]{1,0:T(8,128)S(1)} %add.206), channel_id=1, source_target_pairs={{0,8},{2,10},{4,12},{6,14},{8,0},{10,2},{12,4},{14,6},{16,24},{18,... | collective-permute-start | bytes 196616 | tf_op jit(solution)/shard_map/ppermute | solution.py:21
  173.2 5.2 %collective-permute-start.27 = (f32[128,128]{1,0:T(8,128)S(1)}, f32[128,128]{1,0:T(8,128)S(1)}, u32[]{:S(2)}, u32[]{:S(2)}) collective-permute-start(f32[128,128]{1,0:T(8,128)S(1)} %add.207), channel_id=1, source_target_pairs={{0,16},{2,18},{4,20},{6,22},{8,24},{10,26},{12,28},{14,30},{16,0},... | collective-permute-start | bytes 196616 | tf_op jit(solution)/shard_map/ppermute | solution.py:21
  206.9 4.4 %collective-permute-start.31 = (f32[128]{0:T(128)S(1)}, f32[128]{0:T(128)S(1)}, u32[]{:S(2)}, u32[]{:S(2)}) collective-permute-start(f32[128]{0:T(128)S(1)} %add.211), channel_id=1, source_target_pairs={{0,16},{2,18},{4,20},{6,22},{8,24},{10,26},{12,28},{14,30},{16,0},... | collective-permute-start | bytes 1544 | tf_op jit(solution)/shard_map/ppermute | solution.py:21
  214.2 5.0 %collective-permute-start.32 = (bf16[2,256,128]{1,2,0:T(8,128)(2,1)S(1)}, bf16[2,256,128]{1,2,0:T(8,128)(2,1)S(1)}, u32[]{:S(2)}, u32[]{:S(2)}) collective-permute-start(bf16[2,256,128]{1,2,0:T(8,128)(2,1)S(1)} %get-tuple-element.29), channel_id=1, source_target_pairs={{0,2},{2,0},{4,6},{6,4},{8,10},{10,8},{12,14},{14,12},{16,18},{18,... | collective-permute-start | bytes 393224 | tf_op jit(solution)/shard_map/ppermute | solution.py:21
  215.5 6.7 %collective-permute-start.33 = (bf16[2,256,128]{1,2,0:T(8,128)(2,1)}, bf16[2,256,128]{1,2,0:T(8,128)(2,1)}, u32[]{:S(2)}, u32[]{:S(2)}) collective-permute-start(bf16[2,256,128]{1,2,0:T(8,128)(2,1)} %get-tuple-element.32), channel_id=1, source_target_pairs={{0,4},{2,6},{4,0},{6,2},{8,12},{10,14},{12,8},{14,10},{16,20},{18,... | collective-permute-start | bytes 393224 | tf_op jit(solution)/shard_map/ppermute | solution.py:21
  216.3 9.6 %collective-permute-start.34 = (bf16[2,256,128]{1,2,0:T(8,128)(2,1)}, bf16[2,256,128]{1,2,0:T(8,128)(2,1)}, u32[]{:S(2)}, u32[]{:S(2)}) collective-permute-start(bf16[2,256,128]{1,2,0:T(8,128)(2,1)} %get-tuple-element.31), channel_id=1, source_target_pairs={{0,8},{2,10},{4,12},{6,14},{8,0},{10,2},{12,4},{14,6},{16,24},{18,... | collective-permute-start | bytes 393224 | tf_op jit(solution)/shard_map/ppermute | solution.py:21
  217.9 11.8 %collective-permute-start.35 = (bf16[2,256,128]{1,2,0:T(8,128)(2,1)}, bf16[2,256,128]{1,2,0:T(8,128)(2,1)S(1)}, u32[]{:S(2)}, u32[]{:S(2)}) collective-permute-start(bf16[2,256,128]{1,2,0:T(8,128)(2,1)} %get-tuple-element.30), channel_id=1, source_target_pairs={{0,16},{2,18},{4,20},{6,22},{8,24},{10,26},{12,28},{14,30},{16,0},... | collective-permute-start | bytes 393224 | tf_op jit(solution)/shard_map/ppermute | solution.py:21
  253.0 4.4 %collective-permute-start.39 = (f32[128]{0:T(128)S(1)}, f32[128]{0:T(128)S(1)}, u32[]{:S(2)}, u32[]{:S(2)}) collective-permute-start(f32[128]{0:T(128)S(1)} %add.217), channel_id=1, source_target_pairs={{0,16},{2,18},{4,20},{6,22},{8,24},{10,26},{12,28},{14,30},{16,0},... | collective-permute-start | bytes 1544 | tf_op jit(solution)/shard_map/ppermute | solution.py:21
  (37 other events, 401.7 us)
Sparse Core Ops, SparseCore 0:
  47.5 6.6 all-gather.4
  92.7 7.4 all-gather.6
  137.7 7.5 all-gather.8
  215.6 7.4 all-gather.10
